TPU v7x, 32 devices: a whole 2x2x4 slice. The times are simulated.
32 devices in a mesh: wide: 32 (over z, y, x, core), narrow: 1.
Axes of the slice: x: 2, y: 2, z: 4, core: 2. Of those that a mesh axis runs over, the one named last changes fastest.
Arguments:
- field: float32 [256, 44, 512], P('wide', 'narrow')
- sketch_one: float32 [512, 128], replicated, may hold values from -6 to 6
- sketch_two: float32 [256, 128], replicated, may hold values from -6 to 6
- ranks: int32 [2], replicated, may hold values from 64 to 128, as said below
Outputs:
- core: float32 [128, 44, 128], P('wide', 'narrow')
Inputs may be any that keep to these rules, and one draw needn't show every extreme that they name: One of the two ranks equals 128.
All inputs are finite; a program needn't handle non-finite values.
Results may differ from a plain program's by a relative error of at most 0.00022.
Values sent between devices are 32-bit elements; how exact they have to be, the bound alone decides.
A program may use at most 64 MiB of HBM per device.

v0:
```python
import jax
import jax.numpy as jnp
from jax import lax
from jax.sharding import PartitionSpec as P


def combine(partial_sum):
    return lax.psum(partial_sum, ("wide", "narrow"))


def make_basis(local, sketch, rank):
    highest = lax.Precision.HIGHEST
    keep = (jnp.arange(sketch.shape[1]) < rank).astype(jnp.float32)
    masked = sketch * keep
    partial_gram = jnp.einsum("akn,akm->nm", local, local, precision=highest)
    sketched = jnp.dot(combine(partial_gram), masked, precision=highest)
    inner = jnp.dot(sketched.T, sketched, precision=highest) + jnp.diag(1.0 - keep)
    lower = jnp.linalg.cholesky(inner)
    return jax.scipy.linalg.solve_triangular(lower, sketched.T, lower=True)


def per_device(field, sketch_one, sketch_two, ranks):
    highest = lax.Precision.HIGHEST
    basis_one = make_basis(field, sketch_one, ranks[0])
    core_one = jnp.einsum("rn,ykn->rky", basis_one, field, precision=highest)
    regrouped = lax.all_to_all(core_one, "wide", split_axis=0, concat_axis=2, tiled=True)
    basis_two = make_basis(regrouped, sketch_two, ranks[1])
    return jnp.einsum("sn,rkn->rks", basis_two, regrouped, precision=highest)


def solution(mesh):
    return jax.shard_map(
        per_device,
        mesh=mesh,
        in_specs=(P("wide", "narrow", None), P(), P(), P()),
        out_specs=P("wide", "narrow", None),
        check_vma=False,
    )
```

profile of v0, /device:TPU:0, one launch (start us, length us, event | category | flops | bytes accessed | tf_op | source)
XLA Modules:
  0.0 346.2 jit_solution(5141929274860126565)
XLA Ops:
  6.5 0.0 copy-start
  6.5 0.0 all-reduce.3.cloned.1.call-start
  6.5 1.1 copy-done
  7.6 2.9 convolution_bitcast_fusion
  10.5 0.0 copy-start.3
  10.5 0.0 copy-start.1
  10.5 0.0 all-reduce.3.cloned.1.call-update
  10.6 0.0 all-reduce.5.cloned.1.call-start
  10.6 0.6 copy-done.3
  11.2 0.6 fusion.20
  11.8 0.6 compare_convert_fusion.1
  12.4 0.6 broadcast_subtract_fusion.1
  13.0 132.1 %all-reduce.3.cloned.1.call-done = f32[512,512]{1,0:T(8,128)} async-done(((f32[512,512]{1,0:T(8,128)}), f32[512,512]{1,0:T(8,128)}) %all-reduce.3.cloned.1.call-update) | async-done | bytes 1048592 | tf_op jit(solution)/shard_map/psum | solution.py:8
  145.2 0.0 copy-done.1
  145.2 2.2 fusion.6
  147.4 0.6 convolution_add_fusion.1
  148.0 0.1 copy.21
  148.1 0.1 copy.22
  148.2 11.7 %cholesky.44 = f32[128,128]{1,0:T(8,128)S(1)} custom-call(f32[128,128]{1,0:T(8,128)S(1)} %copy.22), custom_call_target="Cholesky" | custom-call | tf_op jit(solution)/shard_map/jit(cholesky)/cholesky | solution.py:18
  159.9 0.7 compare_reduce_fusion.1
  160.7 0.7 fusion.11
  161.4 9.8 %custom-call.10 = f32[1,128,128]{1,2,0:T(8,128)S(1)} custom-call(f32[1,128,128]{2,1,0:T(8,128)S(1)} %fusion.11), custom_call_target="InvertDiagBlocksLowerTriangular" | custom-call | tf_op jit(solution)/shard_map/jit(_solve_triangular)/triangular_solve | solution.py:19
  171.2 0.4 convolution_bitcast_fusion.2
  171.6 1.1 convolution_bitcast_fusion.3
  172.7 0.2 copy.24
  172.9 0.6 reshape.39
  173.6 12.1 %all_to_all.18 = f32[32,1,1408]{2,1,0:T(1,128)S(1)} all-to-all(f32[32,1,1408]{2,1,0:T(1,128)S(1)} %reshape.39), channel_id=1, replica_groups=mesh['wide'=32,'narrow'=1] {'wide'}, dimensions={0} | all-to-all | bytes 360448 | tf_op jit(solution)/shard_map/all_to_all | solution.py:26
  185.7 0.6 broadcast.90
  186.3 1.1 reduce.4
  187.4 0.7 reshape.40
  188.1 1.3 convolution_bitcast_fusion.1
  189.4 0.0 copy-start.2
  189.4 0.0 all-reduce.5.cloned.1.call-update
  189.4 0.7 compare_convert_fusion
  190.1 0.7 broadcast_subtract_fusion
  190.8 121.8 %all-reduce.5.cloned.1.call-done = f32[256,256]{1,0:T(8,128)} async-done(((f32[256,256]{1,0:T(8,128)}), f32[256,256]{1,0:T(8,128)}) %all-reduce.5.cloned.1.call-update) | async-done | bytes 262160 | tf_op jit(solution)/shard_map/psum | solution.py:8
  312.6 0.0 copy-done.2
  312.6 1.3 fusion.8
  313.9 0.4 convolution_add_fusion
  314.3 0.1 copy.28
  314.4 0.1 copy.29
  314.5 11.7 %cholesky.55 = f32[128,128]{1,0:T(8,128)S(1)} custom-call(f32[128,128]{1,0:T(8,128)S(1)} %copy.29), custom_call_target="Cholesky" | custom-call | tf_op jit(solution)/shard_map/jit(cholesky)/cholesky | solution.py:18
  326.3 0.6 compare_reduce_fusion
  326.9 0.7 fusion.12
  327.6 9.8 %custom-call.11 = f32[1,128,128]{1,2,0:T(8,128)S(1)} custom-call(f32[1,128,128]{2,1,0:T(8,128)S(1)} %fusion.12), custom_call_target="InvertDiagBlocksLowerTriangular" | custom-call | tf_op jit(solution)/shard_map/jit(_solve_triangular)/triangular_solve | solution.py:19
  337.4 0.3 convolution_bitcast_fusion.4
  337.7 1.0 fusion.1
  338.7 0.7 copy.31
  (4 shorter events, 0.1 us)
Async XLA Ops:
  6.5 1.1 copy-start
  6.5 138.6 %all-reduce.3.cloned.1.call-start = ((), (), s32[]{:S(2)}) async-start(), calls=%async_computation.1 | async-start | bytes 2097152 | tf_op jit(solution)/shard_map/psum | solution.py:8
  10.5 0.7 copy-start.3
  10.5 134.6 %copy-start.1 = (f32[512,128]{1,0:T(8,128)S(1)}, f32[512,128]{1,0:T(8,128)}, u32[]{:S(2)}) copy-start(f32[512,128]{1,0:T(8,128)} %param.6) | copy-start | bytes 786436
  10.6 302.0 %all-reduce.5.cloned.1.call-start = ((), (), s32[]{:S(2)}) async-start(), calls=%async_computation.2 | async-start | bytes 524288 | tf_op jit(solution)/shard_map/psum | solution.py:8
  189.4 123.2 %copy-start.2 = (f32[256,128]{1,0:T(8,128)S(1)}, f32[256,128]{1,0:T(8,128)}, u32[]{:S(2)}) copy-start(f32[256,128]{1,0:T(8,128)} %param.7) | copy-start | bytes 393220
Sparse Core Ops, SparseCore 0:
  12.5 132.5 all-reduce.2
  189.5 122.9 all-reduce.4
where the time goes:
time: 347 us; the launch traced here: 346 us
  waiting for transfers between devices  254 us (73%)
  other arithmetic  49.5 us (14%)
  between operations  13.6 us (4%)
  blocking collectives  12.1 us (3%)
  matrix products  11.5 us (3%)
  local copies, waits for them, and re-layouts  5.47 us (2%)
    psum x2, waiting for transfers between devices, combine(): return lax.psum(partial_sum, ('wide', 'narrow'))  254 us
    another operation x6, other arithmetic, make_basis(): lower = jnp.linalg.cholesky(inner)  24.9 us
    another operation x4, other arithmetic, make_basis(): return jax.scipy.linalg.solve_triangular(lower, sketched.T, lower=True)  21 us
    all_to_all x1, blocking collectives, per_device(): lax.all_to_all(core_one, 'wide', split_axis=0, concat_axis=2, tiled=True)  12.1 us
  transfers between devices with their start and end apart: 2, of which 2 were waited for; matrix products, arithmetic and copies ran while one was open for 1% of the time, Pallas kernels for 0%

commit v1 on v0

--- a/solution.py
+++ b/solution.py
@@ -23,7 +23,10 @@
     highest = lax.Precision.HIGHEST
     basis_one = make_basis(field, sketch_one, ranks[0])
     core_one = jnp.einsum("rn,ykn->rky", basis_one, field, precision=highest)
-    regrouped = lax.all_to_all(core_one, "wide", split_axis=0, concat_axis=2, tiled=True)
+    size = lax.axis_size("wide")
+    blocks = jnp.stack(jnp.split(core_one, size, axis=0), axis=0)
+    blocks = lax.all_to_all(blocks, "wide", split_axis=0, concat_axis=0)
+    regrouped = jnp.concatenate(blocks, axis=2)
     basis_two = make_basis(regrouped, sketch_two, ranks[1])
     return jnp.einsum("sn,rkn->rks", basis_two, regrouped, precision=highest)
 

time: 347 us -> 360 us (1.037)
  local copies, waits for them, and re-layouts: 5.47 us -> 19.2 us
    another operation x0 -> x35, local copies, waits for them, and re-layouts: none -> 7.9 us  [per_device(): blocks = jnp.stack(jnp.split(core_one, size, axis=0), axis=0)]
    unnamed x10 -> x77, local copies, waits for them, and re-layouts: 3.02 us -> 9.14 us
where the time goes in v1:
time: 360 us
  waiting for transfers between devices  254 us (71%)
  other arithmetic  49.5 us (14%)
  local copies, waits for them, and re-layouts  19.2 us (5%)
  between operations  13.9 us (4%)
  blocking collectives  12.1 us (3%)
  matrix products  11.5 us (3%)
    psum x2, waiting for transfers between devices, combine(): return lax.psum(partial_sum, ('wide', 'narrow'))  254 us
    another operation x6, other arithmetic, make_basis(): lower = jnp.linalg.cholesky(inner)  24.8 us
    another operation x4, other arithmetic, make_basis(): return jax.scipy.linalg.solve_triangular(lower, sketched.T, lower=True)  20.9 us
    all_to_all x1, blocking collectives, per_device(): blocks = lax.all_to_all(blocks, 'wide', split_axis=0, concat_axis=0)  12.1 us
    unnamed x77, local copies, waits for them, and re-layouts  9.14 us
    another operation x35, local copies, waits for them, and re-layouts, per_device(): blocks = jnp.stack(jnp.split(core_one, size, axis=0), axis=0)  7.9 us
  transfers between devices with their start and end apart: 2, of which 2 were waited for; matrix products, arithmetic and copies ran while one was open for 1% of the time, Pallas kernels for 0%

profile of v1, /device:TPU:0, one launch (start us, length us, event | category | flops | bytes accessed | tf_op | source)
XLA Modules:
  0.0 359.9 jit_solution(6705686926650443269)
XLA Ops:
  6.5 1.1 copy-done
  7.6 2.9 convolution_bitcast_fusion
  10.6 0.6 copy-done.21
  11.2 0.6 fusion.20
  11.8 0.7 broadcast_subtract_fusion.1
  12.4 0.7 compare_convert_fusion.1
  13.1 131.9 %all-reduce.3.cloned.1.call-done = f32[512,512]{1,0:T(8,128)} async-done(((f32[512,512]{1,0:T(8,128)}), f32[512,512]{1,0:T(8,128)}) %all-reduce.3.cloned.1.call-update) | async-done | bytes 1048592 | tf_op jit(solution)/shard_map/psum | solution.py:8
  145.1 2.2 fusion.6
  147.3 0.6 convolution_add_fusion.1
  148.1 11.7 %cholesky.44 = f32[128,128]{1,0:T(8,128)S(1)} custom-call(f32[128,128]{1,0:T(8,128)S(1)} %copy.52), custom_call_target="Cholesky" | custom-call | tf_op jit(solution)/shard_map/jit(cholesky)/cholesky | solution.py:18
  159.9 0.7 compare_reduce_fusion.1
  160.5 0.6 fusion.11
  161.2 9.8 %custom-call.10 = f32[1,128,128]{1,2,0:T(8,128)S(1)} custom-call(f32[1,128,128]{2,1,0:T(8,128)S(1)} %fusion.11), custom_call_target="InvertDiagBlocksLowerTriangular" | custom-call | tf_op jit(solution)/shard_map/jit(_solve_triangular)/triangular_solve | solution.py:19
  171.0 0.4 convolution_bitcast_fusion.2
  171.4 1.1 convolution_bitcast_fusion.3
  172.5 0.7 slice_bitcast_fusion.19
  173.2 2.8 slice_bitcast_fusion
  176.2 0.1 copy.64
  176.3 0.1 copy.63
  177.5 0.1 copy.55
  177.7 0.7 copy-done.18
  178.7 0.7 copy-done.16
  179.6 0.7 copy-done.14
  180.6 0.7 copy-done.12
  181.5 0.7 copy-done.10
  182.5 0.7 copy-done.8
  183.3 0.3 copy.74
  183.6 0.5 copy-done.6
  184.4 0.7 copy-done.4
  185.3 0.7 copy-done.2
  186.8 0.6 reshape.47
  187.4 12.1 %all_to_all.5 = f32[32,1,1408]{2,1,0:T(1,128)S(1)} all-to-all(f32[32,1,1408]{2,1,0:T(1,128)S(1)} %reshape.47), channel_id=1, replica_groups=mesh['wide'=32,'narrow'=1] {'wide'}, dimensions={0} | all-to-all | bytes 360448 | tf_op jit(solution)/shard_map/all_to_all | solution.py:28
  199.5 0.5 broadcast.90
  200.1 1.1 reduce.4
  201.1 0.7 reshape.48
  201.8 1.3 convolution_bitcast_fusion.1
  203.2 0.7 broadcast_subtract_fusion
  203.9 0.7 compare_convert_fusion
  204.5 121.8 %all-reduce.5.cloned.1.call-done = f32[256,256]{1,0:T(8,128)} async-done(((f32[256,256]{1,0:T(8,128)}), f32[256,256]{1,0:T(8,128)}) %all-reduce.5.cloned.1.call-update) | async-done | bytes 262160 | tf_op jit(solution)/shard_map/psum | solution.py:8
  326.3 1.3 fusion.8
  327.6 0.4 convolution_add_fusion
  328.2 11.7 %cholesky.55 = f32[128,128]{1,0:T(8,128)S(1)} custom-call(f32[128,128]{1,0:T(8,128)S(1)} %copy.90), custom_call_target="Cholesky" | custom-call | tf_op jit(solution)/shard_map/jit(cholesky)/cholesky | solution.py:18
  340.0 0.6 compare_reduce_fusion
  340.6 0.7 fusion.12
  341.3 9.8 %custom-call.11 = f32[1,128,128]{1,2,0:T(8,128)S(1)} custom-call(f32[1,128,128]{2,1,0:T(8,128)S(1)} %fusion.12), custom_call_target="InvertDiagBlocksLowerTriangular" | custom-call | tf_op jit(solution)/shard_map/jit(_solve_triangular)/triangular_solve | solution.py:19
  351.1 0.3 convolution_bitcast_fusion.4
  351.4 1.0 fusion.1
  352.4 0.7 copy.92
  (105 shorter events, 4.7 us)
Async XLA Ops:
  6.5 1.1 copy-start
  6.5 138.5 %all-reduce.3.cloned.1.call-start = ((), (), s32[]{:S(2)}) async-start(), calls=%async_computation.1 | async-start | bytes 2097152 | tf_op jit(solution)/shard_map/psum | solution.py:8
  10.5 0.7 copy-start.21
  10.5 134.5 %copy-start.19 = (f32[512,128]{1,0:T(8,128)S(1)}, f32[512,128]{1,0:T(8,128)}, u32[]{:S(2)}) copy-start(f32[512,128]{1,0:T(8,128)} %param.6) | copy-start | bytes 786436
  10.6 315.7 %all-reduce.5.cloned.1.call-start = ((), (), s32[]{:S(2)}) async-start(), calls=%async_computation.2 | async-start | bytes 524288 | tf_op jit(solution)/shard_map/psum | solution.py:8
  177.5 0.9 copy-start.18
  177.6 1.0 copy-start.17
  178.4 0.9 copy-start.16
  178.6 0.9 copy-start.15
  179.3 0.9 copy-start.14
  179.5 0.9 copy-start.13
  180.3 0.9 copy-start.12
  180.5 0.9 copy-start.11
  181.2 0.9 copy-start.10
  181.4 0.9 copy-start.9
  182.2 0.9 copy-start.8
  182.4 0.9 copy-start.7
  183.2 0.9 copy-start.6
  183.3 0.9 copy-start.5
  184.1 0.9 copy-start.4
  184.3 0.9 copy-start.3
  185.1 0.9 copy-start.2
  185.2 0.9 copy-start.1
  203.1 123.1 %copy-start.20 = (f32[256,128]{1,0:T(8,128)S(1)}, f32[256,128]{1,0:T(8,128)}, u32[]{:S(2)}) copy-start(f32[256,128]{1,0:T(8,128)} %param.7) | copy-start | bytes 393220
Sparse Core Ops, SparseCore 0:
  12.5 132.4 all-reduce.2
  203.3 122.9 all-reduce.4

commit v2 on v0

--- a/solution.py
+++ b/solution.py
@@ -5,7 +5,7 @@
 
 
 def combine(partial_sum):
-    return lax.psum(partial_sum, ("wide", "narrow"))
+    return lax.all_gather(partial_sum, axis_name=("wide", "narrow")).sum(axis=0)
 
 
 def make_basis(local, sketch, rank):

time: 347 us -> 375 us (1.081)
  other arithmetic: 49.5 us -> 65.7 us
  waiting for transfers between devices: 254 us -> 269 us
    all_gather x0 -> x2, waiting for transfers between devices: none -> 269 us  [combine(): return lax.all_gather(partial_sum, axis_name=('wide', 'narrow')).sum(axis=0)]
    psum x2 -> x0, waiting for transfers between devices: 254 us -> none  [combine(): return lax.psum(partial_sum, ('wide', 'narrow'))]
    reduce_sum x0 -> x2, other arithmetic: none -> 16.2 us  [combine(): return lax.all_gather(partial_sum, axis_name=('wide', 'narrow')).sum(axis=0)]
where the time goes in v2:
time: 375 us
  waiting for transfers between devices  269 us (72%)
  other arithmetic  65.7 us (18%)
  between operations  13.6 us (4%)
  blocking collectives  11.3 us (3%)
  matrix products  9.29 us (2%)
  local copies, waits for them, and re-layouts  5.62 us (1%)
    all_gather x2, waiting for transfers between devices, combine(): return lax.all_gather(partial_sum, axis_name=('wide', 'narrow')).sum(axis=0)  269 us
    another operation x6, other arithmetic, make_basis(): lower = jnp.linalg.cholesky(inner)  24.9 us
    another operation x4, other arithmetic, make_basis(): return jax.scipy.linalg.solve_triangular(lower, sketched.T, lower=True)  21 us
    reduce_sum x2, other arithmetic, combine(): return lax.all_gather(partial_sum, axis_name=('wide', 'narrow')).sum(axis=0)  16.2 us
    all_to_all x1, blocking collectives, per_device(): lax.all_to_all(core_one, 'wide', split_axis=0, concat_axis=2, tiled=True)  11.3 us
  transfers between devices with their start and end apart: 2, of which 2 were waited for; matrix products, arithmetic and copies ran while one was open for 1% of the time, Pallas kernels for 0%

profile of v2, /device:TPU:0, one launch (start us, length us, event | category | flops | bytes accessed | tf_op | source)
XLA Modules:
  0.0 374.8 jit_solution(3805061560455757645)
XLA Ops:
  6.5 0.0 copy-start
  6.5 0.0 copy-start.1
  6.5 0.0 copy-start.2
  6.5 0.0 all-gather.5.cloned.1.call-start
  6.5 1.1 copy-done
  7.6 2.8 convolution_bitcast_fusion
  10.5 0.0 all-gather.5.cloned.1.call-update
  10.5 0.0 all-gather.7.cloned.1.call-start
  10.6 1.3 fusion.20
  11.9 0.6 compare_convert_fusion.1
  12.5 0.6 broadcast_subtract_fusion.1
  13.2 195.0 %all-gather.5.cloned.1.call-done = f32[16384,512]{1,0:T(8,128)} async-done(((f32[512,512]{1,0:T(8,128)}), f32[16384,512]{1,0:T(8,128)}) %all-gather.5.cloned.1.call-update) | async-done | bytes 33554448 | tf_op jit(solution)/shard_map/all_gather | solution.py:8
  208.2 12.3 %reduce_sum.18 = f32[512,512]{1,0:T(8,128)S(1)} reduce(f32[32,512,512]{2,1,0:T(8,128)} %bitcast.54, f32[]{:T(128)} %constant.43.clone.1), dimensions={0}, to_apply=%region_0.0 | reduce | flops 8126464 | bytes 34603012 | tf_op jit(solution)/shard_map/reduce_sum | solution.py:8
  220.4 0.0 copy-done.1
  220.4 1.0 fusion.6
  221.4 0.6 convolution_add_fusion.1
  222.0 0.1 copy.27
  222.1 0.1 copy.28
  222.2 11.7 %cholesky.44 = f32[128,128]{1,0:T(8,128)S(1)} custom-call(f32[128,128]{1,0:T(8,128)S(1)} %copy.28), custom_call_target="Cholesky" | custom-call | tf_op jit(solution)/shard_map/jit(cholesky)/cholesky | solution.py:18
  234.0 0.7 compare_reduce_fusion.1
  234.7 0.7 fusion.11
  235.4 9.8 %custom-call.10 = f32[1,128,128]{1,2,0:T(8,128)S(1)} custom-call(f32[1,128,128]{2,1,0:T(8,128)S(1)} %fusion.11), custom_call_target="InvertDiagBlocksLowerTriangular" | custom-call | tf_op jit(solution)/shard_map/jit(_solve_triangular)/triangular_solve | solution.py:19
  245.2 0.4 convolution_bitcast_fusion.2
  245.7 1.1 convolution_bitcast_fusion.3
  246.7 0.2 copy.30
  247.0 0.6 reshape.41
  247.6 11.3 %all_to_all.18 = f32[32,1,1408]{2,1,0:T(1,128)S(1)} all-to-all(f32[32,1,1408]{2,1,0:T(1,128)S(1)} %reshape.41), channel_id=1, replica_groups=mesh['wide'=32,'narrow'=1] {'wide'}, dimensions={0} | all-to-all | bytes 360448 | tf_op jit(solution)/shard_map/all_to_all | solution.py:26
  258.9 0.6 broadcast.90
  259.5 1.1 reduce.4
  260.6 0.7 reshape.42
  261.3 1.3 convolution_bitcast_fusion.1
  262.7 0.0 all-gather.7.cloned.1.call-update
  262.7 0.7 compare_convert_fusion
  263.4 0.7 broadcast_subtract_fusion
  264.0 74.2 %all-gather.7.cloned.1.call-done = f32[8192,256]{1,0:T(8,128)} async-done(((f32[256,256]{1,0:T(8,128)}), f32[8192,256]{1,0:T(8,128)}) %all-gather.7.cloned.1.call-update) | async-done | bytes 8388624 | tf_op jit(solution)/shard_map/all_gather | solution.py:8
  338.2 3.9 %reduce_sum.19 = f32[256,256]{1,0:T(8,128)S(1)} reduce(f32[32,256,256]{2,1,0:T(8,128)} %bitcast.55, f32[]{:T(128)} %constant.43.clone.1), dimensions={0}, to_apply=%region_3.5 | reduce | flops 2031616 | bytes 8650756 | tf_op jit(solution)/shard_map/reduce_sum | solution.py:8
  342.1 0.0 copy-done.2
  342.1 0.4 fusion.8
  342.5 0.4 convolution_add_fusion
  342.9 0.1 copy.34
  343.0 0.1 copy.35
  343.1 11.7 %cholesky.55 = f32[128,128]{1,0:T(8,128)S(1)} custom-call(f32[128,128]{1,0:T(8,128)S(1)} %copy.35), custom_call_target="Cholesky" | custom-call | tf_op jit(solution)/shard_map/jit(cholesky)/cholesky | solution.py:18
  354.9 0.6 compare_reduce_fusion
  355.5 0.7 fusion.12
  356.2 9.8 %custom-call.11 = f32[1,128,128]{1,2,0:T(8,128)S(1)} custom-call(f32[1,128,128]{2,1,0:T(8,128)S(1)} %fusion.12), custom_call_target="InvertDiagBlocksLowerTriangular" | custom-call | tf_op jit(solution)/shard_map/jit(_solve_triangular)/triangular_solve | solution.py:19
  366.0 0.3 convolution_bitcast_fusion.4
  366.3 1.0 fusion.1
  367.3 0.7 copy.37
  (4 shorter events, 0.1 us)
Async XLA Ops:
  6.5 1.1 copy-start
  6.5 213.9 %copy-start.1 = (f32[512,128]{1,0:T(8,128)S(1)}, f32[512,128]{1,0:T(8,128)}, u32[]{:S(2)}) copy-start(f32[512,128]{1,0:T(8,128)} %param.6) | copy-start | bytes 786436
  6.5 335.6 %copy-start.2 = (f32[256,128]{1,0:T(8,128)S(1)}, f32[256,128]{1,0:T(8,128)}, u32[]{:S(2)}) copy-start(f32[256,128]{1,0:T(8,128)} %param.7) | copy-start | bytes 393220
  6.5 201.6 %all-gather.5.cloned.1.call-start = ((), (), s32[]{:S(2)}) async-start(), calls=%async_computation.1 | async-start | bytes 34603008 | tf_op jit(solution)/shard_map/all_gather | solution.py:8
  10.5 327.7 %all-gather.7.cloned.1.call-start = ((), (), s32[]{:S(2)}) async-start(), calls=%async_computation.2 | async-start | bytes 8650752 | tf_op jit(solution)/shard_map/all_gather | solution.py:8
Sparse Core Ops, SparseCore 0:
  10.6 197.4 all-gather.4
  262.8 75.3 all-gather.6
